TPU v7x, 256 devices: a whole 4x4x8 slice. The times are simulated.
256 devices in a mesh: group: 16 (over x, y), member: 8 (over z), half: 2 (over core).
Axes of the slice: x: 4, y: 4, z: 8, core: 2. Of those that a mesh axis runs over, the one named last changes fastest.
Arguments:
- tokens: bfloat16 [16384, 2048], P(('group', 'member'), 'half'), may hold values from -6 to 6
- group_ids: int32 [16384, 1], P(('group', 'member')), may hold values from 0 to 15, as said below
- expert_ids: int32 [2, 16384, 4], P(None, ('group', 'member')), may hold values from 0 to 7, as said below
- gate_weights: bfloat16 [2, 16384, 4], P(None, ('group', 'member')), may hold values from 0.25 to 1
- w_gate: bfloat16 [128, 2048, 768], P(('group', 'member'), None, 'half'), may hold values from -0.125 to 0.125
- w_up: bfloat16 [128, 2048, 768], P(('group', 'member'), None, 'half'), may hold values from -0.125 to 0.125
- w_down: bfloat16 [128, 768, 2048], P(('group', 'member'), 'half'), may hold values from -0.21875 to 0.21875
Outputs:
- rows_out: bfloat16 [16384, 2048], P(('group', 'member'), 'half')
Inputs may be any that keep to these rules, and one draw needn't show every extreme that they name: `group_ids`: in each aligned block of 128 rows (the rows of one device) at most 12 rows name the same group, and in every block some group is named by exactly 12 rows. `expert_ids`: each row names four different members. Among the rows of one device that name one group, in one pass, at most 6 name the same member; the rows of one device that take up all 12 slots of a group reach it. Every member is named by some row.
All inputs are finite; a program needn't handle non-finite values.
Results may differ from a plain program's by a relative error of at most 0.015.
Values may be sent and summed in bfloat16 or wider, within the bound.
A program may use at most 64 MiB of HBM per device.

v0:
```python
import jax
import jax.numpy as jnp
from jax import lax
from jax.sharding import PartitionSpec as P

epsilon = 1e-06


def widen_rows(part):
    return lax.all_gather(part, "half", axis=1, tiled=True)


def on_device(tokens, group_ids, expert_ids, gate_weights, w_gate, w_up, w_down):
    groups = lax.axis_size("group")
    members = lax.axis_size("member")
    halves = lax.axis_size("half")
    tok_rows, half_width = tokens.shape
    full_width = half_width * halves
    capacity = 3 * tok_rows // (2 * groups)
    slot_count = groups * capacity
    passes = expert_ids.shape[0]
    column_ids = jnp.arange(groups, dtype=jnp.int32)
    onehot = (group_ids == column_ids[None, :]).astype(jnp.int32)
    before = jnp.cumsum(onehot, axis=0) - onehot
    target = group_ids[:, 0] * capacity + jnp.sum(before * onehot, axis=1)
    placing = jnp.arange(slot_count, dtype=jnp.int32)[:, None] == target[None, :]
    send_rows = jnp.dot(
        placing.astype(jnp.bfloat16), tokens, preferred_element_type=jnp.float32
    ).astype(jnp.bfloat16)
    member_ids = jnp.arange(members, dtype=jnp.int32)
    dense_gates = jnp.sum(
        gate_weights.astype(jnp.float32)[..., None]
        * (expert_ids[..., None] == member_ids).astype(jnp.float32),
        axis=2,
    )
    dense_gates = jnp.transpose(dense_gates, (1, 0, 2)).reshape(tok_rows, passes * members)
    send_gates = jnp.dot(
        placing.astype(jnp.float32), dense_gates, precision=lax.Precision.HIGHEST
    ).astype(jnp.bfloat16)
    landed_rows, landed_gates = (
        lax.all_to_all(
            send_rows.reshape(groups, capacity, half_width),
            "group",
            split_axis=0,
            concat_axis=0,
            tiled=True,
        ),
        lax.all_to_all(
            send_gates.reshape(groups, capacity, passes * members),
            "group",
            split_axis=0,
            concat_axis=0,
            tiled=True,
        ),
    )
    stream = landed_rows.reshape(slot_count, half_width)
    gate_table = landed_gates.reshape(slot_count, passes * members)
    own_member = lax.axis_index("member")
    select = (member_ids == own_member).astype(jnp.float32)
    whole_rows = None
    for pass_index in range(passes):
        whole_rows = widen_rows(stream)

        def expert_rows(pieces, offset, pass_index=pass_index):
            piece_rows, piece_gates = pieces
            gate_column = jnp.sum(
                piece_gates[:, pass_index * members : (pass_index + 1) * members].astype(
                    jnp.float32
                )
                * select,
                axis=1,
            )
            pre_gate = jnp.dot(piece_rows, w_gate[0], preferred_element_type=jnp.float32)
            up_value = jnp.dot(piece_rows, w_up[0], preferred_element_type=jnp.float32)
            hidden = (jax.nn.silu(pre_gate) * up_value).astype(jnp.bfloat16)
            projected = jnp.dot(hidden, w_down[0], preferred_element_type=jnp.float32)
            return (projected * gate_column[:, None]).astype(jnp.bfloat16)

        partials = expert_rows(
            lax.all_gather((whole_rows, gate_table), "member", axis=0, tiled=True), jnp.int32(0)
        )
        blocks = (
            partials.reshape(members, slot_count, halves, half_width)
            .transpose(0, 2, 1, 3)
            .reshape(members * halves * slot_count, half_width)
        )
        summed = lax.psum_scatter(
            blocks, ("member", "half"), scatter_dimension=0, tiled=True
        ).astype(jnp.float32)
        lifted = stream.astype(jnp.float32) + summed
        squares = lax.psum(jnp.sum(lifted * lifted, axis=1), "half")
        stream = (lifted * lax.rsqrt(squares / full_width + epsilon)[:, None]).astype(jnp.bfloat16)
    returned = lax.all_to_all(
        stream.reshape(groups, capacity, half_width),
        "group",
        split_axis=0,
        concat_axis=0,
        tiled=True,
    )
    result = jnp.dot(
        placing.T.astype(jnp.bfloat16),
        returned.reshape(slot_count, half_width),
        preferred_element_type=jnp.float32,
    )
    return result.astype(jnp.bfloat16)


def solution(mesh):
    placed = (
        P(("group", "member"), "half"),
        P(("group", "member"), None),
        P(None, ("group", "member"), None),
        P(None, ("group", "member"), None),
        P(("group", "member"), None, "half"),
        P(("group", "member"), None, "half"),
        P(("group", "member"), "half", None),
    )
    return jax.shard_map(
        on_device,
        mesh=mesh,
        in_specs=placed,
        out_specs=P(("group", "member"), "half"),
        check_vma=False,
    )
```

profile of v0, /device:TPU:1, one launch (start us, length us, event | category | flops | bytes accessed | tf_op | source)
XLA Modules:
  0.0 423.9 jit_solution(2817183692337303223)
XLA Ops:
  9.1 1.2 convolution_convert_fusion
  10.4 17.7 %all_to_all.15 = bf16[16,12,1024]{2,1,0:T(8,128)(2,1)S(1)} all-to-all(bf16[16,12,1024]{2,1,0:T(8,128)(2,1)S(1)} %reshape.52), channel_id=1, replica_groups=mesh['group'=16,'member'=8,'half'=2] {'group'}, dimensions={0} | all-to-all | bytes 786432 | tf_op jit(solution)/shard_map/all_to_all | solution.py:41
  28.2 4.3 %all_gather.16 = bf16[192,2048]{1,0:T(8,128)(2,1)} all-gather(bf16[192,1024]{1,0:T(8,128)(2,1)S(1)} %reshape.53), channel_id=1, replica_groups=mesh['group'=16,'member'=8,'half'=2] {'half'}, dimensions={1}, use_global_device_ids=true | all-gather | bytes 1179648 | tf_op jit(solution)/shard_map/all_gather | solution.py:10
  33.5 3.5 all-to-all-start.1
  37.1 6.4 %all-to-all-done.1 = bf16[16,12,16]{1,2,0:T(8,128)(2,1)S(1)} async-done(((bf16[16,12,16]{1,2,0:T(8,128)(2,1)}), bf16[16,12,16]{1,2,0:T(8,128)(2,1)S(1)}, u32[]{:S(2)}, u32[]{:S(2)}) %all-to-all-start.1) | async-done | bytes 6176 | tf_op jit(solution)/shard_map/all_to_all | solution.py:48
  43.6 24.6 %all-gather = bf16[8,192,16]{1,2,0:T(8,128)(2,1)S(1)} all-gather(bf16[1,192,16]{1,2,0:T(8,128)(2,1)S(1)} %reshape.63), channel_id=1, replica_groups=mesh['group'=16,'member'=8,'half'=2] {'member'}, dimensions={0}, use_global_device_ids=true | all-gather | bytes 55296 | tf_op jit(solution)/shard_map/all_gather | solution.py:80
  68.4 38.4 %all-gather.4.cloned.1.call-done = bf16[1536,2048]{1,0:T(8,128)(2,1)} async-done(((bf16[192,2048]{1,0:T(8,128)(2,1)}), bf16[1536,2048]{1,0:T(8,128)(2,1)}) %all-gather.4.cloned.1.call-update) | async-done | bytes 6291472 | tf_op jit(solution)/shard_map/all_gather | solution.py:80
  106.9 8.1 %fusion.8 = f32[1536,384]{1,0:T(8,128)} fusion(bf16[1536,2048]{1,0:T(8,128)(2,1)} %all-gather.4.cloned.1.call-done, bf16[1,2048,384]{2,1,0:T(8,128)(2,1)} %param.11), kind=kOutput, calls=%fused_computation.12 | convolution fusion | flops 2415919104 | bytes 10223616 | tf_op jit(solution)/shard_map/dot_general | solution.py:73
  115.0 11.3 %multiply_convert_fusion.1 = bf16[1536,2048]{1,0:T(8,128)(2,1)} fusion(f32[1536]{0:T(1024)S(1)} %get-tuple-element.5, bf16[1,384,2048]{2,1,0:T(8,128)(2,1)S(1)} %copy-done, bf16[1536,2048]{1,0:T(8,128)(2,1)} %all-gather.4.cloned.1.call-done, f32[1536,384]{1,0:T(8,128)} %fusion.8, bf16[1,2048,384]{2,1,0:T(8,128)(2,1)} %param.12), kind=kOutput, calls=%fused_computation.1 | convolution fusion | flops 4841668608 | bytes 18094080 | tf_op jit(solution)/shard_map/dot_general | solution.py:76
  126.3 11.1 %reshape.57 = bf16[8,192,2,1024]{3,2,1,0:T(2,128)(2,1)} reshape(bf16[1536,2048]{1,0:T(8,128)(2,1)} %multiply_convert_fusion.1) | data formatting | bytes 12582912 | tf_op jit(solution)/shard_map/reshape | solution.py:83
  137.4 7.5 %copy.25 = bf16[8,192,2,1024]{3,1,2,0:T(8,128)(2,1)} copy(bf16[8,192,2,1024]{3,2,1,0:T(2,128)(2,1)} %reshape.57) | data formatting | bytes 12582912 | tf_op jit(solution)/shard_map/reshape | solution.py:83
  144.9 62.2 %reduce-scatter.3.cloned.1.call-done = bf16[192,1024]{1,0:T(8,128)(2,1)} async-done(((bf16[3072,1024]{1,0:T(8,128)(2,1)}), bf16[192,1024]{1,0:T(8,128)(2,1)}) %reduce-scatter.3.cloned.1.call-update) | async-done | bytes 393232 | tf_op jit(solution)/shard_map/reduce_scatter | solution.py:87
  207.2 1.2 multiply_reduce_fusion.1
  208.4 5.9 %psum.14 = f32[192]{0:T(256)S(1)} all-reduce(f32[192]{0:T(256)S(1)} %multiply_reduce_fusion.1), channel_id=1, replica_groups=mesh['group'=16,'member'=8,'half'=2] {'half'}, use_global_device_ids=true, to_apply=%region_6.7 | all-reduce | flops 192 | bytes 1536 | tf_op jit(solution)/shard_map/psum | solution.py:91
  215.4 2.5 all_gather.19
  218.2 72.7 %all-gather.6.cloned.1.call-done = bf16[1536,2048]{1,0:T(8,128)(2,1)} async-done(((bf16[192,2048]{1,0:T(8,128)(2,1)}), bf16[1536,2048]{1,0:T(8,128)(2,1)}) %all-gather.6.cloned.1.call-update) | async-done | bytes 6291472 | tf_op jit(solution)/shard_map/all_gather | solution.py:80
  290.9 8.1 %fusion.6 = f32[1536,384]{1,0:T(8,128)} fusion(bf16[1536,2048]{1,0:T(8,128)(2,1)} %all-gather.6.cloned.1.call-done, bf16[1,2048,384]{2,1,0:T(8,128)(2,1)} %param.11), kind=kOutput, calls=%fused_computation.10 | convolution fusion | flops 2415919104 | bytes 10223616 | tf_op jit(solution)/shard_map/dot_general | solution.py:73
  299.0 11.3 %multiply_convert_fusion = bf16[1536,2048]{1,0:T(8,128)(2,1)} fusion(f32[1536]{0:T(1024)S(1)} %get-tuple-element.6, bf16[1,384,2048]{2,1,0:T(8,128)(2,1)S(1)} %copy-done, bf16[1536,2048]{1,0:T(8,128)(2,1)} %all-gather.6.cloned.1.call-done, f32[1536,384]{1,0:T(8,128)} %fusion.6, bf16[1,2048,384]{2,1,0:T(8,128)(2,1)} %param.12), kind=kOutput, calls=%fused_computation | convolution fusion | flops 4841668608 | bytes 18094080 | tf_op jit(solution)/shard_map/dot_general | solution.py:76
  310.3 11.1 %reshape.59 = bf16[8,192,2,1024]{3,2,1,0:T(2,128)(2,1)} reshape(bf16[1536,2048]{1,0:T(8,128)(2,1)} %multiply_convert_fusion) | data formatting | bytes 12582912 | tf_op jit(solution)/shard_map/reshape | solution.py:83
  321.4 7.5 %copy.26 = bf16[8,192,2,1024]{3,1,2,0:T(8,128)(2,1)} copy(bf16[8,192,2,1024]{3,2,1,0:T(2,128)(2,1)} %reshape.59) | data formatting | bytes 12582912 | tf_op jit(solution)/shard_map/reshape | solution.py:83
  328.9 62.2 %reduce-scatter.5.cloned.1.call-done = bf16[192,1024]{1,0:T(8,128)(2,1)} async-done(((bf16[3072,1024]{1,0:T(8,128)(2,1)}), bf16[192,1024]{1,0:T(8,128)(2,1)}) %reduce-scatter.5.cloned.1.call-update) | async-done | bytes 393232 | tf_op jit(solution)/shard_map/reduce_scatter | solution.py:87
  391.2 1.2 multiply_reduce_fusion
  392.4 6.0 %psum.15 = f32[192]{0:T(256)S(1)} all-reduce(f32[192]{0:T(256)S(1)} %multiply_reduce_fusion), channel_id=1, replica_groups=mesh['group'=16,'member'=8,'half'=2] {'half'}, use_global_device_ids=true, to_apply=%region_10.11 | all-reduce | flops 192 | bytes 1536 | tf_op jit(solution)/shard_map/psum | solution.py:91
  399.6 16.7 %all_to_all.16 = bf16[16,12,1024]{2,1,0:T(8,128)(2,1)S(1)} all-to-all(bf16[16,12,1024]{2,1,0:T(8,128)(2,1)S(1)} %reshape.61), channel_id=1, replica_groups=mesh['group'=16,'member'=8,'half'=2] {'group'}, dimensions={0} | all-to-all | bytes 786432 | tf_op jit(solution)/shard_map/all_to_all | solution.py:93
  (38 shorter events, 7.9 us)
Async XLA Ops:
  6.5 108.4 %copy-start = (bf16[1,384,2048]{2,1,0:T(8,128)(2,1)S(1)}, bf16[1,384,2048]{2,1,0:T(8,128)(2,1)}, u32[]{:S(2)}) copy-start(bf16[1,384,2048]{2,1,0:T(8,128)(2,1)} %param.13) | copy-start | bytes 4718596
  6.5 100.3 %all-gather.4.cloned.1.call-start = ((), (), s32[]{:S(2)}) async-start(), calls=%async_computation.5 | async-start | bytes 7077888 | tf_op jit(solution)/shard_map/all_gather | solution.py:80
  10.3 22.2 %copy-start.2 = (bf16[2,128,4]{1,2,0:T(4,128)(2,1)S(1)}, bf16[2,128,4]{1,2,0:T(4,128)(2,1)}, u32[]{:S(2)}) copy-start(bf16[2,128,4]{1,2,0:T(4,128)(2,1)} %param.10) | copy-start | bytes 6148
  10.3 22.2 %copy-start.1 = (s32[2,128,4]{1,2,0:T(4,128)S(1)}, s32[2,128,4]{1,2,0:T(4,128)}, u32[]{:S(2)}) copy-start(s32[2,128,4]{1,2,0:T(4,128)} %param.9) | copy-start | bytes 12292
  33.5 10.0 %all-to-all-start.1 = ((bf16[16,12,16]{1,2,0:T(8,128)(2,1)}), bf16[16,12,16]{1,2,0:T(8,128)(2,1)S(1)}, u32[]{:S(2)}, u32[]{:S(2)}) async-start(bf16[16,12,16]{1,2,0:T(8,128)(2,1)} %copy.22), calls=%async_computation.1 | async-start | bytes 131072 | tf_op jit(solution)/shard_map/all_to_all | solution.py:48
  37.0 170.1 %reduce-scatter.3.cloned.1.call-start = ((), (), s32[]{:S(2)}) async-start(), calls=%async_computation.6 | async-start | bytes 6684672 | tf_op jit(solution)/shard_map/reduce_scatter | solution.py:87
  144.9 146.1 %all-gather.6.cloned.1.call-start = ((), (), s32[]{:S(2)}) async-start(), calls=%async_computation.7 | async-start | bytes 7077888 | tf_op jit(solution)/shard_map/all_gather | solution.py:80
  218.0 173.2 %reduce-scatter.5.cloned.1.call-start = ((), (), s32[]{:S(2)}) async-start(), calls=%async_computation.8 | async-start | bytes 6684672 | tf_op jit(solution)/shard_map/reduce_scatter | solution.py:87
Sparse Core Ops, SparseCore 0:
  32.6 74.2 all-gather.3
  145.0 62.1 reduce-scatter.2
  218.1 72.7 all-gather.5
  329.0 62.0 reduce-scatter.4
where the time goes:
time: 425 us; the launch traced here: 424 us
  waiting for transfers between devices  242 us (57%)
  blocking collectives  77.6 us (18%)
  matrix products  41.1 us (10%)
  local copies, waits for them, and re-layouts  38.7 us (9%)
  between operations  13.3 us (3%)
  other arithmetic  7.32 us (2%)
    reduce_scatter x2, waiting for transfers between devices, on_device(): lax.psum_scatter(blocks, ('member', 'half'), scatter_dimension=0, tiled=T...  124 us
    all_gather x2, waiting for transfers between devices, on_device(): lax.all_gather((whole_rows, gate_table), 'member', axis=0, tiled=True)  111 us
    reshape x4, local copies, waits for them, and re-layouts, on_device(): partials.reshape(members, slot_count, halves, half_width)  37.2 us
    all_gather x1, blocking collectives, on_device(): lax.all_gather((whole_rows, gate_table), 'member', axis=0, tiled=True)  24.6 us
    dot_general x2, matrix products, expert_rows(): projected = jnp.dot(hidden, w_down[0], preferred_element_type=jnp.float32)  22.6 us
    all_to_all x1, blocking collectives, on_device(): lax.all_to_all(send_rows.reshape(groups, capacity, half_width), 'group',...  17.7 us
    all_to_all x1, blocking collectives, on_device(): lax.all_to_all(stream.reshape(groups, capacity, half_width), 'group', spl...  16.7 us
    dot_general x2, matrix products, expert_rows(): jnp.dot(piece_rows, w_gate[0], preferred_element_type=jnp.float32)  16.2 us
  transfers between devices with their start and end apart: 5, of which 5 were waited for; matrix products, arithmetic and copies ran while one was open for 0% of the time, Pallas kernels for 0%

commit v1 on v0

v1 whole, which is shorter than its diff:
```python
import functools

import jax
import jax.numpy as jnp
from jax import lax
from jax.experimental import pallas as pl
from jax.experimental.pallas import tpu as pltpu
from jax.sharding import PartitionSpec as P

MESH = pl.DeviceIdType.MESH
BF16 = jnp.bfloat16
F32 = jnp.float32
EPSILON = 1e-6
SUBS = 4
PICKS = 6
TILE = 8
TILES = 3


def first_rows(value):
    return value[0:8]


def turned_dot(left, right):
    return lax.dot_general(left, right, (((0,), (0,)), ((), ())), preferred_element_type=F32)


def kernel(
    tok_ref, gid_ref, eid_ref, gw_ref, wg_hbm, wu_hbm, wd_hbm, out_ref,
    wg, wu, wd, xa, sel, rows_in, part_out, part_in, acc, term_out, term_in, yv, ring_out, ring_in,
    meta_out, meta, lift, sq_out, sq_in,
    w_sem, g_send, g_recv, r_send, r_recv, x_send, x_recv, t_send, t_recv, d_send, d_recv, p_send, p_recv,
    n_send, n_recv, m_send, m_recv,
):
    g = lax.axis_index("group")
    m = lax.axis_index("member")
    h = lax.axis_index("half")
    groups, members = 16, 8
    rows, width = tok_ref.shape
    sub_rows = rows // SUBS

    def place(group=None, member=None, half=None):
        return (
            g if group is None else group,
            m if member is None else member,
            h if half is None else half,
        )

    above = place(member=lax.rem(m + 1, members))
    below = place(member=lax.rem(m + members - 1, members))
    sibling = place(half=1 - h)
    ring_to = (above, below)

    def send(src, dst, send_sem, recv_sem, target):
        return pltpu.make_async_remote_copy(
            src_ref=src, dst_ref=dst, send_sem=send_sem, recv_sem=recv_sem,
            device_id=target, device_id_type=MESH,
        )

    barrier = pltpu.get_barrier_semaphore()

    def greet(target):
        pl.semaphore_signal(barrier, inc=1, device_id=target, device_id_type=MESH)

    greet(sibling)

    def greet_member(d, c):
        greet(place(member=lax.rem(m + d, members)))
        return c

    def greet_group(d, c):
        greet(place(group=lax.rem(g + d, groups)))
        return c

    lax.fori_loop(1, members, greet_member, 0)
    lax.fori_loop(1, groups, greet_group, 0)

    own_k = pl.ds(pl.multiple_of(h * width, width), width)
    other_k = pl.ds(pl.multiple_of((1 - h) * width, width), width)
    weight_copies = [
        pltpu.make_async_copy(wg_hbm.at[0, own_k, :], wg.at[0], w_sem.at[0]),
        pltpu.make_async_copy(wg_hbm.at[0, other_k, :], wg.at[1], w_sem.at[1]),
        pltpu.make_async_copy(wu_hbm.at[0, own_k, :], wu.at[0], w_sem.at[2]),
        pltpu.make_async_copy(wu_hbm.at[0, other_k, :], wu.at[1], w_sem.at[3]),
        pltpu.make_async_copy(wd_hbm.at[0, :, own_k], wd.at[0], w_sem.at[4]),
        pltpu.make_async_copy(wd_hbm.at[0, :, other_k], wd.at[1], w_sem.at[5]),
    ]
    for copy in weight_copies:
        copy.start()

    lane = lax.broadcasted_iota(jnp.int32, (rows, rows), 1)
    down = lax.broadcasted_iota(jnp.int32, (rows, rows), 0)

    def kind(s):
        return lax.rem(m + s, 2)

    def own(s):
        return kind(s) == 0

    def other(s):
        return kind(s) == 1

    def half_subs(way):
        return range(SUBS // 2) if way == 0 else range(SUBS // 2, SUBS)

    def sub_ds(sub):
        return pl.ds(sub * sub_rows, sub_rows)

    def g_copy(p, s, way, msg, sub):
        pi = kind(s)
        if way == 0:
            src, dst = ((0, pi), (1 + pi, 2 + pi))[msg]
        else:
            src, dst = ((pi, 1 + pi), (2 + pi, 3))[msg]
        sp = 2 * p + s
        return send(
            xa.at[p, s, src, sub_ds(sub)], xa.at[p, s, dst, sub_ds(sub)],
            g_send.at[sp, way, msg, sub], g_recv.at[sp, way, msg, sub], ring_to[way],
        )

    def g_wait(p, s, way, msg, sub):
        pi = kind(s)
        if way == 0:
            dst = (1 - pi, 3 - pi)[msg]
        else:
            dst = (2 - pi, 3)[msg]
        sp = 2 * p + s
        pltpu.make_async_copy(
            xa.at[p, s, dst, sub_ds(sub)], xa.at[p, s, dst, sub_ds(sub)], g_recv.at[sp, way, msg, sub]
        ).wait()

    def gather_own(p, s):
        @pl.when(own(s))
        def _():
            for sub in range(SUBS):
                for way in (0, 1):
                    g_copy(p, s, way, 0, sub).start()

    def gather_first(p, s):
        for sub in range(SUBS):
            for way in (0, 1):
                g_wait(p, s, way, 0, sub)

                @pl.when(own(s))
                def _():
                    g_copy(p, s, way, 1, sub).start()

                @pl.when(other(s))
                def _():
                    g_copy(p, s, way, 0, sub).start()

    def gather_second(p, s):
        @pl.when(own(s))
        def _():
            for way in (0, 1):
                for sub in half_subs(way):
                    g_wait(p, s, way, 1, sub)

        @pl.when(other(s))
        def _():
            for i in range(SUBS):
                for way in (0, 1):
                    sub = i if way == 0 else SUBS - 1 - i
                    g_wait(p, s, way, 1, sub)
                    if sub in half_subs(way):
                        g_copy(p, s, way, 1, sub).start()

    def source(s, j):
        pi = kind(s)
        step = (-pi, 3 * pi - 2, 2 - 5 * pi, 4 - pi)[j]
        return lax.rem(m + members + step, members)

    def matches(p, s, k, j):
        record = meta[source(s, j)]
        code = record[p : p + 1, :].astype(jnp.int32)
        gate = record[2 + p : 3 + p, :]
        off = PICKS * j - TILE * k
        at = (code & 7) + off
        good = (code >= 0) & (at >= 0) & (at < TILE)
        return down == jnp.where(good, code + off, -1), gate

    def choose(p, s, k):
        total = None
        for j in (k, k + 1):
            hit, _ = matches(p, s, k, j)
            piece = jnp.dot(
                jnp.where(hit, 1.0, 0.0).astype(BF16), xa[p, s, j], preferred_element_type=F32
            )
            total = piece if total is None else total + piece
        sp = 2 * p + s
        sel[sp, k] = total.astype(BF16).reshape(groups, TILE, width)
        rows_in[sp, k, 0, pl.ds(g, 1)] = sel[sp, k, pl.ds(g, 1)]

        def start(d, c):
            t = lax.rem(g + d, groups)
            send(
                sel.at[sp, k, t], rows_in.at[sp, k, 0, g], x_send.at[sp, k], x_recv.at[sp, k],
                place(group=t),
            ).start()
            return c

        lax.fori_loop(1, groups, start, 0)

    def most(ref, sem):
        part = ref.at[pl.ds(0, groups - 1)]
        pltpu.make_async_copy(part, part, sem).wait()

    def row_copy(p, s, k):
        sp = 2 * p + s
        return send(
            rows_in.at[sp, k, 0], rows_in.at[sp, k, 1], d_send.at[sp, k], d_recv.at[sp, k], sibling
        )

    def landed(p, s, k):
        sp = 2 * p + s
        most(rows_in.at[sp, k, 0], x_recv.at[sp, k])
        row_copy(p, s, k).start()

    def part_copy(p, s, k):
        sp = 2 * p + s
        return send(
            part_out.at[sp, k], part_in.at[sp, k], p_send.at[sp, k], p_recv.at[sp, k], sibling
        )

    def expert(p, s, k):
        sp = 2 * p + s
        row_copy(p, s, k).wait_recv()
        mine = rows_in[sp, k, 0].reshape(rows, width)
        theirs = rows_in[sp, k, 1].reshape(rows, width)
        pre = jnp.dot(mine, wg[0], preferred_element_type=F32)
        pre += jnp.dot(theirs, wg[1], preferred_element_type=F32)
        up = jnp.dot(mine, wu[0], preferred_element_type=F32)
        up += jnp.dot(theirs, wu[1], preferred_element_type=F32)
        hidden = (jax.nn.silu(pre) * up).astype(BF16)
        part_out[sp, k] = jnp.dot(hidden, wd[1], preferred_element_type=F32).astype(BF16)
        part_copy(p, s, k).start()
        acc[k] = jnp.dot(hidden, wd[0], preferred_element_type=F32)

    def give_back(p, s, k):
        sp = 2 * p + s
        part_copy(p, s, k).wait_recv()
        total = acc[k] + part_in[sp, k].astype(F32)
        term_out[sp, k] = total.astype(BF16).reshape(groups, TILE, width)
        term_in[sp, k, pl.ds(g, 1)] = term_out[sp, k, pl.ds(g, 1)]

        def start(d, c):
            t = lax.rem(g + d, groups)
            send(
                term_out.at[sp, k, t], term_in.at[sp, k, g], t_send.at[sp, k], t_recv.at[sp, k],
                place(group=t),
            ).start()
            return c

        lax.fori_loop(1, groups, start, 0)

    def returned(p, s, k):
        sp = 2 * p + s
        most(term_in.at[sp, k], t_recv.at[sp, k])

    def weigh(p, s, j):
        sp = 2 * p + s
        total = None
        for k in (j - 1, j):
            if 0 <= k < TILES:
                hit, gate = matches(p, s, k, j)
                piece = turned_dot(
                    jnp.where(hit, gate, 0.0).astype(BF16), term_in[sp, k].reshape(rows, width)
                )
                total = piece if total is None else total + piece
        yv[s, j] = total

    def r_copy(p, s, way, msg, sub):
        sp = 2 * p + s
        return send(
            ring_out.at[sp, way, msg, sub_ds(sub)], ring_in.at[sp, way, msg, sub_ds(sub)],
            r_send.at[sp, way, msg, sub], r_recv.at[sp, way, msg, sub], ring_to[way],
        )

    def sum_start(p, s):
        sp = 2 * p + s

        @pl.when(own(s))
        def _():
            for i in range(SUBS // 2):
                for way in (0, 1):
                    sub = half_subs(way)[i]
                    ring_out[sp, way, 0, sub_ds(sub)] = yv[s, 3, sub_ds(sub)].astype(BF16)
                    r_copy(p, s, way, 0, sub).start()

    def sum_middle(p, s):
        sp = 2 * p + s

        @pl.when(other(s))
        def _():
            order = [(i, way) for i in range(SUBS) for way in (0, 1)]
            fresh = [x for x in order if x[0] not in half_subs(x[1])]
            for sub, way in fresh + [x for x in order if x not in fresh]:
                value = yv[s, (3, 2)[way], sub_ds(sub)]
                if (sub, way) not in fresh:
                    r_copy(p, s, way, 0, sub).wait_recv()
                    value += ring_in[sp, way, 0, sub_ds(sub)].astype(F32)
                ring_out[sp, way, 0, sub_ds(sub)] = value.astype(BF16)
                r_copy(p, s, way, 0, sub).start()

        @pl.when(own(s))
        def _():
            order = [(i, way) for i in range(SUBS) for way in (0, 1)]
            fresh = [x for x in order if x[0] not in half_subs(x[1])]
            for sub, way in fresh + [x for x in order if x not in fresh]:
                r_copy(p, s, way, 0, sub).wait_recv()
                value = yv[s, (2, 1)[way], sub_ds(sub)] + ring_in[sp, way, 0, sub_ds(sub)].astype(F32)
                ring_out[sp, way, 1, sub_ds(sub)] = value.astype(BF16)
                r_copy(p, s, way, 1, sub).start()

    def sum_last(p, s):
        sp = 2 * p + s

        @pl.when(other(s))
        def _():
            order = [(i, way) for i in range(SUBS) for way in (0, 1)]
            fresh = [x for x in order if x[0] not in half_subs(x[1])]
            for sub, way in fresh + [x for x in order if x not in fresh]:
                r_copy(p, s, way, 1, sub).wait_recv()
                value = yv[s, (1, 0)[way], sub_ds(sub)] + ring_in[sp, way, 1, sub_ds(sub)].astype(F32)
                ring_out[sp, way, 1, sub_ds(sub)] = value.astype(BF16)
                r_copy(p, s, way, 1, sub).start()

    def square_copy(p):
        return send(sq_out.at[p], sq_in.at[p], n_send.at[p], n_recv.at[p], sibling)

    def finish(p, s):
        sp = 2 * p + s

        @pl.when(own(s))
        def _():
            for sub in range(SUBS):
                at = sub_ds(sub)
                for way in (0, 1):
                    r_copy(p, s, way, 1, sub).wait_recv()
                value = xa[p, s, 0, at].astype(F32) + yv[s, 0, at]
                value += ring_in[sp, 0, 1, at].astype(F32) + ring_in[sp, 1, 1, at].astype(F32)
                lift[at] = value
                square = value * value
                part = square[:, 0:128]
                for c in range(128, width, 128):
                    part += square[:, c : c + 128]
                sq_out[p, at] = part
            square_copy(p).start()
            square_copy(p).wait_recv()
            for sub in range(SUBS):
                at = sub_ds(sub)
                mean = jnp.sum(sq_out[p, at] + sq_in[p, at], axis=1, keepdims=True) / (2 * width)
                value = (lift[at] * lax.rsqrt(mean + EPSILON)).astype(BF16)
                if p == 0:
                    xa[1, s, 0, at] = value
                else:
                    out_ref[at] = value

    for s in (0, 1):

        @pl.when(own(s))
        def _():
            xa[0, s, 0] = tok_ref[...]

    pl.semaphore_wait(barrier, groups + members - 1)
    gather_own(0, 0)

    group_of = gid_ref[...]
    onehot = jnp.where(group_of == lane, 1.0, 0.0).astype(BF16)
    same = lax.dot_general(onehot, onehot, (((1,), (1,)), ((), ())), preferred_element_type=F32)
    before = jnp.where(down < lane, same, 0.0).astype(BF16)
    eye = jnp.where(down == lane, 1.0, 0.0).astype(BF16)
    group_row = first_rows(
        turned_dot(jnp.broadcast_to(group_of.astype(F32), (rows, rows)).astype(BF16), eye)
    )
    meta_out[...] = jnp.zeros_like(meta_out)
    for p in (0, 1):
        ids = eid_ref[p]
        weights = gw_ref[p].astype(F32)
        named = jnp.zeros((rows, rows), F32)
        gates = jnp.zeros((rows, rows), F32)
        for c in range(ids.shape[1]):
            hit = ids[:, c : c + 1] == lane
            named += jnp.where(hit, 1.0, 0.0)
            gates += jnp.where(hit, weights[:, c : c + 1], 0.0)
        named = named.astype(BF16)
        rank_row = first_rows(turned_dot(named, before))
        named_row = first_rows(turned_dot(named, eye))
        gate_row = first_rows(turned_dot(gates.astype(BF16), eye))
        code_row = jnp.where(named_row > 0.5, group_row * TILE + rank_row, -1.0)
        for e in range(members):
            meta_out[e, p : p + 1, :] = code_row[e : e + 1]
            meta_out[e, 2 + p : 3 + p, :] = gate_row[e : e + 1]
    meta[pl.ds(m, 1)] = meta_out[pl.ds(m, 1)]

    def send_meta(d, c):
        to = lax.rem(m + d, members)
        send(meta_out.at[to], meta.at[m], m_send.at[0], m_recv.at[0], place(member=to)).start()
        return c

    lax.fori_loop(1, members, send_meta, 0)

    def meta_wait(sem):
        part = meta.at[pl.ds(0, members - 1)]
        pltpu.make_async_copy(part, part, sem.at[0]).wait()

    for p in (0, 1):
        gather_first(p, 0)
        gather_own(p, 1)
        if p == 0:
            meta_wait(m_recv)
        choose(p, 0, 0)
        gather_second(p, 0)
        choose(p, 0, 1)
        choose(p, 0, 2)
        landed(p, 0, 0)
        gather_first(p, 1)
        if p == 0:
            for copy in weight_copies:
                copy.wait()
        expert(p, 0, 0)
        landed(p, 0, 1)
        choose(p, 1, 0)
        give_back(p, 0, 0)
        landed(p, 0, 2)
        expert(p, 0, 1)
        gather_second(p, 1)
        choose(p, 1, 1)
        expert(p, 0, 2)
        give_back(p, 0, 1)
        choose(p, 1, 2)
        give_back(p, 0, 2)
        landed(p, 1, 0)
        returned(p, 0, 0)
        returned(p, 0, 1)
        landed(p, 1, 1)
        returned(p, 0, 2)
        weigh(p, 0, 3)
        sum_start(p, 0)
        weigh(p, 0, 2)
        weigh(p, 0, 1)
        expert(p, 1, 0)
        sum_middle(p, 0)
        landed(p, 1, 2)
        weigh(p, 0, 0)
        give_back(p, 1, 0)
        expert(p, 1, 1)
        sum_last(p, 0)
        expert(p, 1, 2)
        give_back(p, 1, 1)
        give_back(p, 1, 2)
        returned(p, 1, 0)
        returned(p, 1, 1)
        returned(p, 1, 2)
        weigh(p, 1, 3)
        sum_start(p, 1)
        weigh(p, 1, 2)
        finish(p, 0)
        if p == 0:
            gather_own(1, 0)
        weigh(p, 1, 1)
        sum_middle(p, 1)
        weigh(p, 1, 0)
        sum_last(p, 1)
        finish(p, 1)

    meta_wait(m_send)
    for p in (0, 1):
        square_copy(p).wait_send()
        for s in (0, 1):
            sp = 2 * p + s
            for k in range(TILES):
                most(sel.at[sp, k], x_send.at[sp, k])
                most(term_out.at[sp, k], t_send.at[sp, k])
                row_copy(p, s, k).wait_send()
                part_copy(p, s, k).wait_send()
            for way in (0, 1):
                for sub in range(SUBS):
                    g_copy(p, s, way, 0, sub).wait_send()
                    r_copy(p, s, way, 1, sub).wait_send()
                    if sub in half_subs(way):
                        g_copy(p, s, way, 1, sub).wait_send()
                        r_copy(p, s, way, 0, sub).wait_send()
                    else:

                        @pl.when(own(s))
                        def _():
                            g_copy(p, s, way, 1, sub).wait_send()

                        @pl.when(other(s))
                        def _():
                            r_copy(p, s, way, 0, sub).wait_send()


def on_device(tokens, group_ids, expert_ids, gate_weights, w_gate, w_up, w_down):
    rows, width = tokens.shape
    hidden = w_gate.shape[2]
    tile = (16, TILE, width)
    block = (rows, width)
    vmem = pl.BlockSpec(memory_space=pltpu.VMEM)
    anywhere = pl.BlockSpec(memory_space=pl.ANY)
    dma = pltpu.SemaphoreType.DMA
    return pl.pallas_call(
        kernel,
        out_shape=jax.ShapeDtypeStruct(block, BF16),
        in_specs=[vmem] * 4 + [anywhere] * 3,
        out_specs=vmem,
        scratch_shapes=[
            pltpu.VMEM((2, width, hidden), BF16),
            pltpu.VMEM((2, width, hidden), BF16),
            pltpu.VMEM((2, hidden, width), BF16),
            pltpu.VMEM((2, 2, 4, *block), BF16),
            pltpu.VMEM((4, TILES, *tile), BF16),
            pltpu.VMEM((4, TILES, 2, *tile), BF16),
            pltpu.VMEM((4, TILES, *block), BF16),
            pltpu.VMEM((4, TILES, *block), BF16),
            pltpu.VMEM((TILES, *block), F32),
            pltpu.VMEM((4, TILES, *tile), BF16),
            pltpu.VMEM((4, TILES, *tile), BF16),
            pltpu.VMEM((2, 4, *block), F32),
            pltpu.VMEM((4, 2, 2, *block), BF16),
            pltpu.VMEM((4, 2, 2, *block), BF16),
            pltpu.VMEM((8, 8, 128), F32),
            pltpu.VMEM((8, 8, 128), F32),
            pltpu.VMEM(block, F32),
            pltpu.VMEM((2, rows, 128), F32),
            pltpu.VMEM((2, rows, 128), F32),
            dma((6,)),
            dma((4, 2, 2, SUBS)),
            dma((4, 2, 2, SUBS)),
            dma((4, 2, 2, SUBS)),
            dma((4, 2, 2, SUBS)),
            dma((4, TILES)),
            dma((4, TILES)),
            dma((4, TILES)),
            dma((4, TILES)),
            dma((4, TILES)),
            dma((4, TILES)),
            dma((4, TILES)),
            dma((4, TILES)),
            dma((2,)),
            dma((2,)),
            dma((1,)),
            dma((1,)),
        ],
        compiler_params=pltpu.CompilerParams(
            collective_id=0, has_side_effects=True, vmem_limit_bytes=60 * 1024 * 1024
        ),
    )(tokens, group_ids, expert_ids, gate_weights, w_gate, w_up, w_down)


def solution(mesh):
    placed = (
        P(("group", "member"), "half"),
        P(("group", "member"), None),
        P(None, ("group", "member"), None),
        P(None, ("group", "member"), None),
        P(("group", "member"), None, "half"),
        P(("group", "member"), None, "half"),
        P(("group", "member"), "half", None),
    )
    return jax.shard_map(
        on_device,
        mesh=mesh,
        in_specs=placed,
        out_specs=P(("group", "member"), "half"),
        check_vma=False,
    )
```

time: 425 us -> 207 us (0.49)
  waiting for transfers between devices: 242 us -> 0 us
  Pallas kernels: 0 us -> 199 us
  blocking collectives: 77.6 us -> 0 us
  matrix products: 41.1 us -> 0 us
  local copies, waits for them, and re-layouts: 38.7 us -> 5.96 us
  between operations: 13.3 us -> 0.01 us
  other arithmetic: 7.32 us -> 0 us
    pallas_call x0 -> x1, Pallas kernels: none -> 199 us  [on_device(): pl.pallas_call(kernel, out_shape=jax.ShapeDtypeStruct(block, BF16), in_sp...]
    reduce_scatter x2 -> x0, waiting for transfers between devices: 124 us -> none  [on_device(): lax.psum_scatter(blocks, ('member', 'half'), scatter_dimension=0, tiled=T...]
    all_gather x2 -> x0, waiting for transfers between devices: 111 us -> none  [on_device(): lax.all_gather((whole_rows, gate_table), 'member', axis=0, tiled=True)]
    dot_general x7 -> x0, matrix products: 41.1 us -> none  [the longest x2 22.6 us: expert_rows(): projected = jnp.dot(hidden, w_down[0], preferred_element_type=jnp.float32)]
    reshape x10 -> x0, local copies, waits for them, and re-layouts: 38.4 us -> none  [the longest x4 37.2 us: on_device(): partials.reshape(members, slot_count, halves, half_width)]
    all_to_all x2 -> x0, blocking collectives: 34.4 us -> none  [the longest x1 17.7 us: on_device(): lax.all_to_all(send_rows.reshape(groups, capacity, half_width), 'group',...]
    all_gather x3 -> x0, blocking collectives: 31.3 us -> none  [the longest x1 24.6 us: on_device(): lax.all_gather((whole_rows, gate_table), 'member', axis=0, tiled=True)]
    psum x2 -> x0, blocking collectives: 11.9 us -> none  [on_device(): squares = lax.psum(jnp.sum(lifted * lifted, axis=1), 'half')]
  transfers between devices with their start and end apart: 5 -> 0, of which waited for: 5 -> 0; matrix products, arithmetic and copies ran while one was open for 0% -> 0% of each run, Pallas kernels for 0% -> 0%
where the time goes in v1:
time: 207 us; the launch traced here: 205 us
  Pallas kernels  199 us (96%)
  local copies, waits for them, and re-layouts  5.96 us (3%)
    pallas_call x1, Pallas kernels, on_device(): pl.pallas_call(kernel, out_shape=jax.ShapeDtypeStruct(block, BF16), in_sp...  199 us
    unnamed x4, local copies, waits for them, and re-layouts  5.96 us

profile of v1, /device:TPU:1, one launch (start us, length us, event | category | flops | bytes accessed | tf_op | source)
XLA Modules:
  0.0 204.8 jit_solution(8993408370260444760)
XLA Ops:
  0.0 1.4 copy.8.gid_ref
  1.4 1.4 copy.10.gw_ref
  2.8 1.5 copy.9.eid_ref
  4.3 198.8 %shard_map.73 = bf16[128,1024]{1,0:T(8,128)(2,1)} custom-call(bf16[128,1024]{1,0:T(8,128)(2,1)} %tok_ref.1, s32[128,1]{1,0:T(8,128)} %copy.8.gid_ref, s32[2,128,4]{2,1,0:T(8,128)} %copy.9.eid_ref, bf16[2,128,4]{2,1,0:T(8,128)(2,1)} %copy.10.gw_ref, bf16[1,2048,384]{2,1,0:T(8,128)(2,1)} %wg_hbm.1, bf16[1,2048,384]{2,1,0:T(8,128)(2,1)} %wu_hbm.1, ...), custom_call_target="tpu_custom_call" | custom-call | tf_op jit(solution)/shard_map/pallas_call | solution.py:503
  203.1 1.7 copy.12

commit v2 on v0

v2 whole, which is shorter than its diff:
```python
import jax
import jax.numpy as jnp
from jax import lax
from jax.experimental import pallas as pl
from jax.experimental.pallas import tpu as pltpu
from jax.sharding import PartitionSpec as P

MESH = pl.DeviceIdType.MESH
BF16 = jnp.bfloat16
F32 = jnp.float32
EPSILON = 1e-6
TILE = 8
TILES = 6
LAST = TILES - 1
CUTS = 4
BLOCKS = 8
STEP_OF_BLOCK = (0, -1, 1, -2, 2, -3, 3, 4)
FILL = (
    ((0, 0, 0, 4), (1, 4, 4, 8)),
    ((1, -4, 0, 2), (2, 2, 2, 8)),
    ((3, 0, 0, 6), (4, 6, 6, 8)),
    ((4, -2, 0, 4), (5, 4, 4, 8)),
    ((5, -4, 0, 2), (6, 2, 2, 8)),
    ((7, 0, 0, 6), (0, 2, 6, 8)),
)
FAR = ((0, 2), (1, 3))
NEAR = ((1, 3), (0, 2))


def first_rows(value):
    return value[0:8]


def turned_dot(left, right):
    return lax.dot_general(left, right, (((0,), (0,)), ((), ())), preferred_element_type=F32)


def kernel(
    tok_ref, gid_ref, eid_ref, gw_ref, wg_hbm, wu_hbm, wd_hbm, out_ref,
    wg, wu, wd, xa, sel, rows_in, part_out, part_in, acc, term_out, term_in, yv, ring_out, ring_in,
    meta_out, meta, lift, sq_out, sq_in,
    w_sem, g_send, g_recv, r_send, r_recv, x_send, x_recv, t_send, t_recv, d_send, d_recv, p_send, p_recv,
    n_send, n_recv, m_send, m_recv,
):
    g = lax.axis_index("group")
    m = lax.axis_index("member")
    h = lax.axis_index("half")
    groups, members = 16, 8
    rows, width = tok_ref.shape
    cut = width // CUTS

    def place(group=None, member=None, half=None):
        return (
            g if group is None else group,
            m if member is None else member,
            h if half is None else half,
        )

    above = place(member=lax.rem(m + 1, members))
    below = place(member=lax.rem(m + members - 1, members))
    sibling = place(half=1 - h)
    ring_to = (above, below)

    def send(src, dst, send_sem, recv_sem, target):
        return pltpu.make_async_remote_copy(
            src_ref=src, dst_ref=dst, send_sem=send_sem, recv_sem=recv_sem,
            device_id=target, device_id_type=MESH,
        )

    barrier = pltpu.get_barrier_semaphore()

    def greet(target):
        pl.semaphore_signal(barrier, inc=1, device_id=target, device_id_type=MESH)

    greet(sibling)

    def greet_member(d, c):
        greet(place(member=lax.rem(m + d, members)))
        return c

    def greet_group(d, c):
        greet(place(group=lax.rem(g + d, groups)))
        return c

    lax.fori_loop(1, members, greet_member, 0)
    lax.fori_loop(1, groups, greet_group, 0)

    own_k = pl.ds(pl.multiple_of(h * width, width), width)
    other_k = pl.ds(pl.multiple_of((1 - h) * width, width), width)
    weight_copies = [
        pltpu.make_async_copy(wg_hbm.at[0, own_k, :], wg.at[0], w_sem.at[0]),
        pltpu.make_async_copy(wg_hbm.at[0, other_k, :], wg.at[1], w_sem.at[1]),
        pltpu.make_async_copy(wu_hbm.at[0, own_k, :], wu.at[0], w_sem.at[2]),
        pltpu.make_async_copy(wu_hbm.at[0, other_k, :], wu.at[1], w_sem.at[3]),
        pltpu.make_async_copy(wd_hbm.at[0, :, own_k], wd.at[0], w_sem.at[4]),
        pltpu.make_async_copy(wd_hbm.at[0, :, other_k], wd.at[1], w_sem.at[5]),
    ]
    for copy in weight_copies:
        copy.start()

    lane = lax.broadcasted_iota(jnp.int32, (rows, rows), 1)
    down = lax.broadcasted_iota(jnp.int32, (rows, rows), 0)


    def lanes(c):
        return pl.ds(c * cut, cut)

    def g_copy(p, step, way, c):
        src = 0 if step == 1 else 2 * step - 3 + way
        dst = 7 if step == 4 else 2 * step - 1 + way
        return send(
            xa.at[p, src, c], xa.at[p, dst, c],
            g_send.at[p, step - 1, way, c], g_recv.at[p, step - 1, way, c], ring_to[way],
        )

    def gather_start(p):
        for i in range(CUTS):
            for way in (0, 1):
                g_copy(p, 1, way, (FAR[way] + NEAR[way])[i]).start()

    def gather(p, step, which):
        for i in which:
            for way in (0, 1):
                c = (FAR[way] + NEAR[way])[i]
                g_copy(p, step, way, c).wait_recv()
                if step < 3 or (step == 3 and i < 2):
                    g_copy(p, step + 1, way, c).start()

    def matches(p, k, filling):
        j, off, low, high = filling
        record = meta[lax.rem(m + members + STEP_OF_BLOCK[j], members)]
        code = record[p : p + 1, :].astype(jnp.int32)
        gate = record[2 + p : 3 + p, :]
        at = (code & 7) + off
        good = (code >= 0) & (at >= low) & (at < high)
        return down == jnp.where(good, code + off, -1), gate

    def parts_of(k):
        return (0, 1) if k == LAST else (None,)

    def cuts_of(f):
        return range(CUTS) if f is None else range(2 * f, 2 * f + 2)

    def sem_of(f):
        return 0 if f is None else f

    def piece(ref, f):
        return ref if f is None else ref.at[pl.ds(2 * f, 2)]

    def pieces(ref, f):
        return ref if f is None else ref.at[:, pl.ds(2 * f, 2)]

    def choose(p, k, f=None):
        picks = []
        for filling in FILL[k]:
            hit, _ = matches(p, k, filling)
            picks.append((jnp.where(hit, 1.0, 0.0).astype(BF16), filling[0]))
        for c in cuts_of(f):
            total = sum(
                jnp.dot(pick, xa[p, j, c], preferred_element_type=F32) for pick, j in picks
            )
            sel[p, k, :, c] = total.astype(BF16).reshape(groups, TILE, cut)
            rows_in[p, k, 0, pl.ds(g, 1), c] = sel[p, k, pl.ds(g, 1), c]

        def start(d, carry):
            t = lax.rem(g + d, groups)
            send(
                piece(sel.at[p, k, t], f), piece(rows_in.at[p, k, 0, g], f),
                x_send.at[p, k, sem_of(f)], x_recv.at[p, k, sem_of(f)], place(group=t),
            ).start()
            return carry

        lax.fori_loop(1, groups, start, 0)

    def most(ref, sem, f):
        part = ref.at[pl.ds(0, groups - 1)] if f is None else ref.at[pl.ds(0, groups - 1), pl.ds(2 * f, 2)]
        pltpu.make_async_copy(part, part, sem).wait()

    def row_copy(p, k, f=None):
        return send(
            pieces(rows_in.at[p, k, 0], f), pieces(rows_in.at[p, k, 1], f),
            d_send.at[p, k, sem_of(f)], d_recv.at[p, k, sem_of(f)], sibling,
        )

    def landed(p, k, f=None):
        most(rows_in.at[p, k, 0], x_recv.at[p, k, sem_of(f)], f)
        row_copy(p, k, f).start()

    def part_copy(p, k, f=None):
        return send(
            piece(part_out.at[p, k], f), piece(part_in.at[p, k], f),
            p_send.at[p, k, sem_of(f)], p_recv.at[p, k, sem_of(f)], sibling,
        )

    def expert(p, k):
        pre = jnp.zeros((rows, wg.shape[2]), F32)
        up = jnp.zeros((rows, wg.shape[2]), F32)
        for f in parts_of(k):
            row_copy(p, k, f).wait_recv()
            for side in (0, 1):
                for c in cuts_of(f):
                    some = rows_in[p, k, side, :, c].reshape(rows, cut)
                    pre += jnp.dot(some, wg[side, lanes(c), :], preferred_element_type=F32)
                    up += jnp.dot(some, wu[side, lanes(c), :], preferred_element_type=F32)
        hidden = (jax.nn.silu(pre) * up).astype(BF16)
        for f in parts_of(k):
            for c in cuts_of(f):
                part_out[p, k, c] = jnp.dot(
                    hidden, wd[1, :, lanes(c)], preferred_element_type=F32
                ).astype(BF16)
            part_copy(p, k, f).start()
        for c in range(CUTS):
            acc[k, c] = jnp.dot(hidden, wd[0, :, lanes(c)], preferred_element_type=F32)

    def give_back(p, k, f=None):
        part_copy(p, k, f).wait_recv()
        for c in cuts_of(f):
            total = acc[k, c] + part_in[p, k, c].astype(F32)
            term_out[p, k, :, c] = total.astype(BF16).reshape(groups, TILE, cut)
            term_in[p, k, pl.ds(g, 1), c] = term_out[p, k, pl.ds(g, 1), c]

        def start(d, carry):
            t = lax.rem(g + d, groups)
            send(
                piece(term_out.at[p, k, t], f), piece(term_in.at[p, k, g], f),
                t_send.at[p, k, sem_of(f)], t_recv.at[p, k, sem_of(f)], place(group=t),
            ).start()
            return carry

        lax.fori_loop(1, groups, start, 0)

    def returned(p, k, f=None):
        most(term_in.at[p, k], t_recv.at[p, k, sem_of(f)], f)

    def weigh(p, j, f=None):
        picks = []
        for k in range(TILES):
            for filling in FILL[k]:
                if filling[0] == j:
                    hit, gate = matches(p, k, filling)
                    picks.append((jnp.where(hit, gate, 0.0).astype(BF16), k))
        for c in cuts_of(f):
            yv[j, c] = sum(
                turned_dot(pick, term_in[p, k, :, c].reshape(rows, cut)) for pick, k in picks
            )

    def r_copy(p, msg, way, c):
        return send(
            ring_out.at[p, msg, way, c], ring_in.at[p, msg, way, c],
            r_send.at[p, msg, way, c], r_recv.at[p, msg, way, c], ring_to[way],
        )

    def pass_on(p, msg, way, c, add):
        value = yv[7 if msg == 0 else 8 - 2 * msg - way, c]
        if add:
            r_copy(p, msg - 1, way, c).wait_recv()
            value += ring_in[p, msg - 1, way, c].astype(F32)
        ring_out[p, msg, way, c] = value.astype(BF16)
        r_copy(p, msg, way, c).start()

    def sum_far(p, f):
        for way in (0, 1):
            pass_on(p, 0, way, FAR[way][f], False)

    def sum_fresh(p):
        for i in (0, 1):
            for way in (0, 1):
                pass_on(p, 1, way, NEAR[way][i], False)

    def sum_join(p):
        for i in (0, 1):
            for way in (0, 1):
                pass_on(p, 1, way, FAR[way][i], True)

    def sum_on(p, msg):
        for i in range(CUTS):
            for way in (0, 1):
                pass_on(p, msg, way, (NEAR[way] + FAR[way])[i], True)

    def square_copy(p):
        return send(sq_out.at[p], sq_in.at[p], n_send.at[p], n_recv.at[p], sibling)

    def finish(p):
        squares = jnp.zeros((rows, 128), F32)
        for c in (0, 1, 2, 3):
            value = xa[p, 0, c].astype(F32) + yv[0, c]
            for way in (0, 1):
                r_copy(p, 3, way, c).wait_recv()
                value += ring_in[p, 3, way, c].astype(F32)
            lift[c] = value
            square = value * value
            for i in range(0, cut, 128):
                squares += square[:, i : i + 128]
        sq_out[p] = squares
        square_copy(p).start()
        square_copy(p).wait_recv()
        mean = jnp.sum(sq_out[p] + sq_in[p], axis=1, keepdims=True) / (2 * width)
        scale = lax.rsqrt(mean + EPSILON)
        for c in range(CUTS):
            value = (lift[c] * scale).astype(BF16)
            if p == 0:
                xa[1, 0, c] = value
            else:
                out_ref[:, lanes(c)] = value

    for c in range(CUTS):
        xa[0, 0, c] = tok_ref[:, lanes(c)]
    pl.semaphore_wait(barrier, groups + members - 1)
    gather_start(0)

    group_of = gid_ref[...]
    onehot = jnp.where(group_of == lane, 1.0, 0.0).astype(BF16)
    same = lax.dot_general(onehot, onehot, (((1,), (1,)), ((), ())), preferred_element_type=F32)
    before = jnp.where(down < lane, same, 0.0).astype(BF16)
    eye = jnp.where(down == lane, 1.0, 0.0).astype(BF16)
    group_row = first_rows(
        turned_dot(jnp.broadcast_to(group_of.astype(F32), (rows, rows)).astype(BF16), eye)
    )
    meta_out[...] = jnp.zeros_like(meta_out)
    for p in (0, 1):
        ids = eid_ref[p]
        weights = gw_ref[p].astype(F32)
        named = jnp.zeros((rows, rows), F32)
        gates = jnp.zeros((rows, rows), F32)
        for c in range(ids.shape[1]):
            hit = ids[:, c : c + 1] == lane
            named += jnp.where(hit, 1.0, 0.0)
            gates += jnp.where(hit, weights[:, c : c + 1], 0.0)
        named = named.astype(BF16)
        rank_row = first_rows(turned_dot(named, before))
        named_row = first_rows(turned_dot(named, eye))
        gate_row = first_rows(turned_dot(gates.astype(BF16), eye))
        code_row = jnp.where(named_row > 0.5, group_row * TILE + rank_row, -1.0)
        for e in range(members):
            meta_out[e, p : p + 1, :] = code_row[e : e + 1]
            meta_out[e, 2 + p : 3 + p, :] = gate_row[e : e + 1]
    meta[pl.ds(m, 1)] = meta_out[pl.ds(m, 1)]

    def send_meta(d, c):
        to = lax.rem(m + d, members)
        send(meta_out.at[to], meta.at[m], m_send.at[0], m_recv.at[0], place(member=to)).start()
        return c

    lax.fori_loop(1, members, send_meta, 0)

    def meta_wait(sem):
        part = meta.at[pl.ds(0, members - 1)]
        pltpu.make_async_copy(part, part, sem.at[0]).wait()

    for p in (0, 1):
        gather(p, 1, range(CUTS))
        if p == 0:
            meta_wait(m_recv)
        choose(p, 0)
        choose(p, 1)
        gather(p, 2, range(CUTS))
        choose(p, 2)
        landed(p, 0)
        gather(p, 3, (0, 1))
        landed(p, 1)
        if p == 0:
            for copy in weight_copies:
                copy.wait()
        gather(p, 3, (2, 3))
        choose(p, 3)
        choose(p, 4)
        expert(p, 0)
        gather(p, 4, (0,))
        choose(p, LAST, 0)
        gather(p, 4, (1,))
        choose(p, LAST, 1)
        landed(p, 2)
        expert(p, 1)
        expert(p, 2)
        landed(p, 3)
        expert(p, 3)
        give_back(p, 3)
        landed(p, 4)
        expert(p, 4)
        give_back(p, 4)
        landed(p, LAST, 0)
        landed(p, LAST, 1)
        expert(p, LAST)
        give_back(p, LAST, 0)
        give_back(p, LAST, 1)
        give_back(p, 2)
        give_back(p, 1)
        give_back(p, 0)
        returned(p, 3)
        returned(p, 4)
        weigh(p, 6)
        weigh(p, 5)
        sum_fresh(p)
        returned(p, LAST, 0)
        weigh(p, 7, 0)
        sum_far(p, 0)
        returned(p, LAST, 1)
        weigh(p, 7, 1)
        sum_far(p, 1)
        sum_join(p)
        returned(p, 2)
        weigh(p, 4)
        weigh(p, 3)
        sum_on(p, 2)
        returned(p, 1)
        returned(p, 0)
        weigh(p, 2)
        weigh(p, 1)
        weigh(p, 0)
        sum_on(p, 3)
        finish(p)
        if p == 0:
            gather_start(1)

    meta_wait(m_send)
    for p in (0, 1):
        square_copy(p).wait_send()
        for k in range(TILES):
            for f in parts_of(k):
                most(sel.at[p, k], x_send.at[p, k, sem_of(f)], f)
                most(term_out.at[p, k], t_send.at[p, k, sem_of(f)], f)
                row_copy(p, k, f).wait_send()
                part_copy(p, k, f).wait_send()
        for i in range(4):
            for way in (0, 1):
                for c in range(CUTS):
                    if i < 3 or c in FAR[way]:
                        g_copy(p, i + 1, way, c).wait_send()
                        r_copy(p, 3 - i, way, c).wait_send()


def on_device(tokens, group_ids, expert_ids, gate_weights, w_gate, w_up, w_down):
    rows, width = tokens.shape
    hidden = w_gate.shape[2]
    cut = width // CUTS
    tile = (16, CUTS, TILE, cut)
    block = (CUTS, rows, cut)
    vmem = pl.BlockSpec(memory_space=pltpu.VMEM)
    anywhere = pl.BlockSpec(memory_space=pl.ANY)
    dma = pltpu.SemaphoreType.DMA
    return pl.pallas_call(
        kernel,
        out_shape=jax.ShapeDtypeStruct((rows, width), BF16),
        in_specs=[vmem] * 4 + [anywhere] * 3,
        out_specs=vmem,
        scratch_shapes=[
            pltpu.VMEM((2, width, hidden), BF16),
            pltpu.VMEM((2, width, hidden), BF16),
            pltpu.VMEM((2, hidden, width), BF16),
            pltpu.VMEM((2, BLOCKS, *block), BF16),
            pltpu.VMEM((2, TILES, *tile), BF16),
            pltpu.VMEM((2, TILES, 2, *tile), BF16),
            pltpu.VMEM((2, TILES, *block), BF16),
            pltpu.VMEM((2, TILES, *block), BF16),
            pltpu.VMEM((TILES, *block), F32),
            pltpu.VMEM((2, TILES, *tile), BF16),
            pltpu.VMEM((2, TILES, *tile), BF16),
            pltpu.VMEM((BLOCKS, *block), F32),
            pltpu.VMEM((2, 4, 2, *block), BF16),
            pltpu.VMEM((2, 4, 2, *block), BF16),
            pltpu.VMEM((8, 8, 128), F32),
            pltpu.VMEM((8, 8, 128), F32),
            pltpu.VMEM(block, F32),
            pltpu.VMEM((2, rows, 128), F32),
            pltpu.VMEM((2, rows, 128), F32),
            dma((6,)),
            dma((2, 4, 2, CUTS)),
            dma((2, 4, 2, CUTS)),
            dma((2, 4, 2, CUTS)),
            dma((2, 4, 2, CUTS)),
        ]
        + [dma((2, TILES, 2))] * 8
        + [dma((2,)), dma((2,)), dma((1,)), dma((1,))],
        compiler_params=pltpu.CompilerParams(
            collective_id=0, has_side_effects=True, vmem_limit_bytes=60 * 1024 * 1024
        ),
    )(tokens, group_ids, expert_ids, gate_weights, w_gate, w_up, w_down)


def solution(mesh):
    placed = (
        P(("group", "member"), "half"),
        P(("group", "member"), None),
        P(None, ("group", "member"), None),
        P(None, ("group", "member"), None),
        P(("group", "member"), None, "half"),
        P(("group", "member"), None, "half"),
        P(("group", "member"), "half", None),
    )
    return jax.shard_map(
        on_device,
        mesh=mesh,
        in_specs=placed,
        out_specs=P(("group", "member"), "half"),
        check_vma=False,
    )
```

time: 425 us -> 153 us (0.36)
  waiting for transfers between devices: 242 us -> 0 us
  Pallas kernels: 0 us -> 147 us
  blocking collectives: 77.6 us -> 0 us
  matrix products: 41.1 us -> 0 us
  local copies, waits for them, and re-layouts: 38.7 us -> 5.96 us
  between operations: 13.3 us -> 0.01 us
  other arithmetic: 7.32 us -> 0 us
    pallas_call x0 -> x1, Pallas kernels: none -> 147 us  [on_device(): pl.pallas_call(kernel, out_shape=jax.ShapeDtypeStruct((rows, width), BF16...]
    reduce_scatter x2 -> x0, waiting for transfers between devices: 124 us -> none  [on_device(): lax.psum_scatter(blocks, ('member', 'half'), scatter_dimension=0, tiled=T...]
    all_gather x2 -> x0, waiting for transfers between devices: 111 us -> none  [on_device(): lax.all_gather((whole_rows, gate_table), 'member', axis=0, tiled=True)]
    dot_general x7 -> x0, matrix products: 41.1 us -> none  [the longest x2 22.6 us: expert_rows(): projected = jnp.dot(hidden, w_down[0], preferred_element_type=jnp.float32)]
    reshape x10 -> x0, local copies, waits for them, and re-layouts: 38.4 us -> none  [the longest x4 37.2 us: on_device(): partials.reshape(members, slot_count, halves, half_width)]
    all_to_all x2 -> x0, blocking collectives: 34.4 us -> none  [the longest x1 17.7 us: on_device(): lax.all_to_all(send_rows.reshape(groups, capacity, half_width), 'group',...]
    all_gather x3 -> x0, blocking collectives: 31.3 us -> none  [the longest x1 24.6 us: on_device(): lax.all_gather((whole_rows, gate_table), 'member', axis=0, tiled=True)]
    psum x2 -> x0, blocking collectives: 11.9 us -> none  [on_device(): squares = lax.psum(jnp.sum(lifted * lifted, axis=1), 'half')]
  transfers between devices with their start and end apart: 5 -> 0, of which waited for: 5 -> 0; matrix products, arithmetic and copies ran while one was open for 0% -> 0% of each run, Pallas kernels for 0% -> 0%
where the time goes in v2:
time: 153 us
  Pallas kernels  147 us (96%)
  local copies, waits for them, and re-layouts  5.96 us (4%)
    pallas_call x1, Pallas kernels, on_device(): pl.pallas_call(kernel, out_shape=jax.ShapeDtypeStruct((rows, width), BF16...  147 us
    unnamed x4, local copies, waits for them, and re-layouts  5.96 us

profile of v2, /device:TPU:1, one launch (start us, length us, event | category | flops | bytes accessed | tf_op | source)
XLA Modules:
  0.0 153.2 jit_solution(14670503758851865586)
XLA Ops:
  0.0 1.4 copy.8.gid_ref
  1.4 1.4 copy.10.gw_ref
  2.8 1.5 copy.9.eid_ref
  4.3 147.2 %shard_map.73 = bf16[128,1024]{1,0:T(8,128)(2,1)} custom-call(bf16[128,1024]{1,0:T(8,128)(2,1)} %tok_ref.1, s32[128,1]{1,0:T(8,128)} %copy.8.gid_ref, s32[2,128,4]{2,1,0:T(8,128)} %copy.9.eid_ref, bf16[2,128,4]{2,1,0:T(8,128)(2,1)} %copy.10.gw_ref, bf16[1,2048,384]{2,1,0:T(8,128)(2,1)} %wg_hbm.1, bf16[1,2048,384]{2,1,0:T(8,128)(2,1)} %wu_hbm.1, ...), custom_call_target="tpu_custom_call" | custom-call | tf_op jit(solution)/shard_map/pallas_call | solution.py:441
  151.5 1.7 %copy.12 = bf16[128,1024]{1,0:T(8,128)(2,1)} copy(bf16[128,1024]{1,0:T(8,128)(2,1)} %shard_map.73) | data formatting | bytes 524288

commit v3 on v2

--- a/solution.py
+++ b/solution.py
@@ -11,24 +11,39 @@
 EPSILON = 1e-6
 TILE = 8
 TILES = 6
-LAST = TILES - 1
 CUTS = 4
 BLOCKS = 8
 STEP_OF_BLOCK = (0, -1, 1, -2, 2, -3, 3, 4)
 FILL = (
-    ((0, 0, 0, 4), (1, 4, 4, 8)),
-    ((1, -4, 0, 2), (2, 2, 2, 8)),
-    ((3, 0, 0, 6), (4, 6, 6, 8)),
-    ((4, -2, 0, 4), (5, 4, 4, 8)),
-    ((5, -4, 0, 2), (6, 2, 2, 8)),
+    ((1, 0, 0, 6), (0, 6, 6, 8)),
+    ((2, 0, 0, 6), (0, 4, 6, 8)),
+    ((3, 0, 0, 4), (4, 4, 4, 8)),
+    ((5, 0, 0, 6), (3, 2, 6, 8)),
+    ((6, 0, 0, 6), (4, 2, 6, 8)),
     ((7, 0, 0, 6), (0, 2, 6, 8)),
+)
+HALVED = 3
+KEPT = (
+    (0, 1, 2, 3), (0, 1, 2, 3), (0, 1, 2, 3),
+    (0, 2, 1, 3), (1, 3, 0, 2), (0, 1, 2, 3),
 )
 FAR = ((0, 2), (1, 3))
 NEAR = ((1, 3), (0, 2))
 
 
-def first_rows(value):
-    return value[0:8]
+PLAN = (
+    ("GO", 0, 0), ("MC", 0, 0), ("M", 0, 0), ("G", 1, 0), ("G", 1, 1), ("G", 1, 2), ("G", 1, 3), ("C", 1, 0),
+    ("G", 2, 1), ("C", 0, 0), ("G", 2, 0), ("G", 2, 2), ("G", 2, 3), ("C", 2, 0), ("G", 3, 1), ("G", 3, 0),
+    ("C", 4, 0), ("G", 3, 2), ("L", 0, 0), ("C", 3, 0), ("G", 3, 3), ("C", 4, 1), ("L", 1, 0), ("C", 3, 1),
+    ("X", 0, 0), ("G", 4, 1), ("L", 4, 0), ("G", 4, 0), ("C", 5, 0), ("L", 4, 1), ("C", 5, 1), ("L", 3, 0),
+    ("L", 3, 1), ("X", 4, 0), ("X", 3, 0), ("B", 4, 0), ("L", 5, 0), ("B", 3, 0), ("L", 5, 1), ("L", 2, 0),
+    ("B", 4, 1), ("X", 5, 0), ("X", 2, 0), ("B", 5, 0), ("B", 5, 1), ("T", 4, 0), ("W", 6, 0), ("T", 3, 0),
+    ("W", 5, 0), ("R", 1, 3), ("B", 3, 1), ("R", 1, 2), ("X", 1, 0), ("T", 4, 1), ("B", 2, 0), ("T", 5, 0),
+    ("W", 7, 0), ("R", 0, 0), ("T", 5, 1), ("W", 7, 1), ("R", 0, 1), ("B", 1, 0), ("T", 3, 1), ("B", 0, 0),
+    ("W", 6, 1), ("W", 5, 1), ("R", 1, 0), ("R", 1, 1), ("T", 2, 0), ("W", 3, 0), ("W", 4, 0), ("R", 2, 2),
+    ("R", 2, 3), ("T", 1, 0), ("R", 2, 1), ("R", 2, 0), ("W", 2, 0), ("T", 0, 0), ("W", 1, 0), ("R", 3, 3),
+    ("R", 3, 1), ("R", 3, 0), ("R", 3, 2), ("W", 0, 0), ("F1", 0, 0), ("F2", 0, 0),
+)
 
 
 def turned_dot(left, right):
@@ -98,7 +113,6 @@
     for copy in weight_copies:
         copy.start()
 
-    lane = lax.broadcasted_iota(jnp.int32, (rows, rows), 1)
     down = lax.broadcasted_iota(jnp.int32, (rows, rows), 0)
 
 
@@ -136,7 +150,7 @@
         return down == jnp.where(good, code + off, -1), gate
 
     def parts_of(k):
-        return (0, 1) if k == LAST else (None,)
+        return (0, 1) if k >= HALVED else (None,)
 
     def cuts_of(f):
         return range(CUTS) if f is None else range(2 * f, 2 * f + 2)
@@ -155,12 +169,12 @@
         for filling in FILL[k]:
             hit, _ = matches(p, k, filling)
             picks.append((jnp.where(hit, 1.0, 0.0).astype(BF16), filling[0]))
-        for c in cuts_of(f):
+        for i in cuts_of(f):
             total = sum(
-                jnp.dot(pick, xa[p, j, c], preferred_element_type=F32) for pick, j in picks
+                jnp.dot(pick, xa[p, j, KEPT[k][i]], preferred_element_type=F32) for pick, j in picks
             )
-            sel[p, k, :, c] = total.astype(BF16).reshape(groups, TILE, cut)
-            rows_in[p, k, 0, pl.ds(g, 1), c] = sel[p, k, pl.ds(g, 1), c]
+            sel[p, k, :, i] = total.astype(BF16).reshape(groups, TILE, cut)
+            rows_in[p, k, 0, pl.ds(g, 1), i] = sel[p, k, pl.ds(g, 1), i]
 
         def start(d, carry):
             t = lax.rem(g + d, groups)
@@ -195,22 +209,23 @@
     def expert(p, k):
         pre = jnp.zeros((rows, wg.shape[2]), F32)
         up = jnp.zeros((rows, wg.shape[2]), F32)
-        for f in parts_of(k):
-            row_copy(p, k, f).wait_recv()
-            for side in (0, 1):
-                for c in cuts_of(f):
-                    some = rows_in[p, k, side, :, c].reshape(rows, cut)
-                    pre += jnp.dot(some, wg[side, lanes(c), :], preferred_element_type=F32)
-                    up += jnp.dot(some, wu[side, lanes(c), :], preferred_element_type=F32)
+        for side in (0, 1):
+            for f in parts_of(k):
+                if side == 1:
+                    row_copy(p, k, f).wait_recv()
+                for i in cuts_of(f):
+                    some = rows_in[p, k, side, :, i].reshape(rows, cut)
+                    pre += jnp.dot(some, wg[side, lanes(KEPT[k][i]), :], preferred_element_type=F32)
+                    up += jnp.dot(some, wu[side, lanes(KEPT[k][i]), :], preferred_element_type=F32)
         hidden = (jax.nn.silu(pre) * up).astype(BF16)
         for f in parts_of(k):
-            for c in cuts_of(f):
-                part_out[p, k, c] = jnp.dot(
-                    hidden, wd[1, :, lanes(c)], preferred_element_type=F32
+            for i in cuts_of(f):
+                part_out[p, k, i] = jnp.dot(
+                    hidden, wd[1, :, lanes(KEPT[k][i])], preferred_element_type=F32
                 ).astype(BF16)
             part_copy(p, k, f).start()
-        for c in range(CUTS):
-            acc[k, c] = jnp.dot(hidden, wd[0, :, lanes(c)], preferred_element_type=F32)
+        for i in range(CUTS):
+            acc[k, i] = jnp.dot(hidden, wd[0, :, lanes(KEPT[k][i])], preferred_element_type=F32)
 
     def give_back(p, k, f=None):
         part_copy(p, k, f).wait_recv()
@@ -239,9 +254,11 @@
                 if filling[0] == j:
                     hit, gate = matches(p, k, filling)
                     picks.append((jnp.where(hit, gate, 0.0).astype(BF16), k))
-        for c in cuts_of(f):
+        some = range(CUTS) if f is None else [KEPT[picks[0][1]][i] for i in cuts_of(f)]
+        for c in some:
             yv[j, c] = sum(
-                turned_dot(pick, term_in[p, k, :, c].reshape(rows, cut)) for pick, k in picks
+                turned_dot(pick, term_in[p, k, :, KEPT[k].index(c)].reshape(rows, cut))
+                for pick, k in picks
             )
 
     def r_copy(p, msg, way, c):
@@ -258,24 +275,9 @@
         ring_out[p, msg, way, c] = value.astype(BF16)
         r_copy(p, msg, way, c).start()
 
-    def sum_far(p, f):
+    def sums(p, msg, u):
         for way in (0, 1):
-            pass_on(p, 0, way, FAR[way][f], False)
-
-    def sum_fresh(p):
-        for i in (0, 1):
-            for way in (0, 1):
-                pass_on(p, 1, way, NEAR[way][i], False)
-
-    def sum_join(p):
-        for i in (0, 1):
-            for way in (0, 1):
-                pass_on(p, 1, way, FAR[way][i], True)
-
-    def sum_on(p, msg):
-        for i in range(CUTS):
-            for way in (0, 1):
-                pass_on(p, msg, way, (NEAR[way] + FAR[way])[i], True)
+            pass_on(p, msg, way, (FAR[way] + NEAR[way])[u], msg > 1 or (msg == 1 and u < 2))
 
     def square_copy(p):
         return send(sq_out.at[p], sq_in.at[p], n_send.at[p], n_recv.at[p], sibling)
@@ -293,6 +295,8 @@
                 squares += square[:, i : i + 128]
         sq_out[p] = squares
         square_copy(p).start()
+
+    def norm(p):
         square_copy(p).wait_recv()
         mean = jnp.sum(sq_out[p] + sq_in[p], axis=1, keepdims=True) / (2 * width)
         scale = lax.rsqrt(mean + EPSILON)
@@ -308,109 +312,79 @@
     pl.semaphore_wait(barrier, groups + members - 1)
     gather_start(0)
 
-    group_of = gid_ref[...]
-    onehot = jnp.where(group_of == lane, 1.0, 0.0).astype(BF16)
-    same = lax.dot_general(onehot, onehot, (((1,), (1,)), ((), ())), preferred_element_type=F32)
-    before = jnp.where(down < lane, same, 0.0).astype(BF16)
-    eye = jnp.where(down == lane, 1.0, 0.0).astype(BF16)
-    group_row = first_rows(
-        turned_dot(jnp.broadcast_to(group_of.astype(F32), (rows, rows)).astype(BF16), eye)
-    )
-    meta_out[...] = jnp.zeros_like(meta_out)
-    for p in (0, 1):
-        ids = eid_ref[p]
-        weights = gw_ref[p].astype(F32)
-        named = jnp.zeros((rows, rows), F32)
-        gates = jnp.zeros((rows, rows), F32)
-        for c in range(ids.shape[1]):
-            hit = ids[:, c : c + 1] == lane
-            named += jnp.where(hit, 1.0, 0.0)
-            gates += jnp.where(hit, weights[:, c : c + 1], 0.0)
-        named = named.astype(BF16)
-        rank_row = first_rows(turned_dot(named, before))
-        named_row = first_rows(turned_dot(named, eye))
-        gate_row = first_rows(turned_dot(gates.astype(BF16), eye))
-        code_row = jnp.where(named_row > 0.5, group_row * TILE + rank_row, -1.0)
-        for e in range(members):
-            meta_out[e, p : p + 1, :] = code_row[e : e + 1]
-            meta_out[e, 2 + p : 3 + p, :] = gate_row[e : e + 1]
-    meta[pl.ds(m, 1)] = meta_out[pl.ds(m, 1)]
-
-    def send_meta(d, c):
-        to = lax.rem(m + d, members)
-        send(meta_out.at[to], meta.at[m], m_send.at[0], m_recv.at[0], place(member=to)).start()
-        return c
-
-    lax.fori_loop(1, members, send_meta, 0)
+    def make_meta():
+        lane = lax.broadcasted_iota(jnp.int32, (rows, rows), 1)
+        number = lax.broadcasted_iota(jnp.int32, (groups, rows), 0)
+        group_of = gid_ref[...]
+        onehot = jnp.where(number == group_of, 1.0, 0.0).astype(BF16)
+        before = jnp.where(down < lane, turned_dot(onehot, onehot), 0.0).astype(BF16)
+        meta_out[...] = jnp.zeros_like(meta_out)
+        for p in (0, 1):
+            ids = eid_ref[p]
+            weights = gw_ref[p].astype(F32)
+            named = jnp.zeros((groups, rows), F32)
+            gates = jnp.zeros((groups, rows), F32)
+            for c in range(ids.shape[0]):
+                hit = number == ids[c : c + 1]
+                named += jnp.where(hit, 1.0, 0.0)
+                gates += jnp.where(hit, weights[c : c + 1], 0.0)
+            rank = jnp.dot(named.astype(BF16), before, preferred_element_type=F32)
+            code = jnp.where(named > 0.5, group_of.astype(F32) * TILE + rank, -1.0)
+            for e in range(members):
+                meta_out[e, p : p + 1, :] = code[e : e + 1]
+                meta_out[e, 2 + p : 3 + p, :] = gates[e : e + 1]
+        meta[pl.ds(m, 1)] = meta_out[pl.ds(m, 1)]
+
+        def send_meta(d, c):
+            to = lax.rem(m + d, members)
+            send(meta_out.at[to], meta.at[m], m_send.at[0], m_recv.at[0], place(member=to)).start()
+            return c
+
+        lax.fori_loop(1, members, send_meta, 0)
 
     def meta_wait(sem):
         part = meta.at[pl.ds(0, members - 1)]
         pltpu.make_async_copy(part, part, sem.at[0]).wait()
 
+    def run(p, name, i, f):
+        part = f if i >= HALVED else None
+        if name == "GO":
+            gather_start(p)
+        elif name == "MC":
+            make_meta()
+        elif name == "M":
+            meta_wait(m_recv)
+        elif name == "G":
+            gather(p, i, (f,))
+        elif name == "C":
+            choose(p, i, part)
+        elif name == "L":
+            landed(p, i, part)
+        elif name == "X":
+            expert(p, i)
+        elif name == "B":
+            give_back(p, i, part)
+        elif name == "T":
+            returned(p, i, part)
+        elif name == "W":
+            weigh(p, i, f if i > 4 else None)
+        elif name == "R":
+            sums(p, i, f)
+        elif name == "F1":
+            finish(p)
+        elif name == "F2":
+            norm(p)
+
     for p in (0, 1):
-        gather(p, 1, range(CUTS))
-        if p == 0:
-            meta_wait(m_recv)
-        choose(p, 0)
-        choose(p, 1)
-        gather(p, 2, range(CUTS))
-        choose(p, 2)
-        landed(p, 0)
-        gather(p, 3, (0, 1))
-        landed(p, 1)
-        if p == 0:
-            for copy in weight_copies:
-                copy.wait()
-        gather(p, 3, (2, 3))
-        choose(p, 3)
-        choose(p, 4)
-        expert(p, 0)
-        gather(p, 4, (0,))
-        choose(p, LAST, 0)
-        gather(p, 4, (1,))
-        choose(p, LAST, 1)
-        landed(p, 2)
-        expert(p, 1)
-        expert(p, 2)
-        landed(p, 3)
-        expert(p, 3)
-        give_back(p, 3)
-        landed(p, 4)
-        expert(p, 4)
-        give_back(p, 4)
-        landed(p, LAST, 0)
-        landed(p, LAST, 1)
-        expert(p, LAST)
-        give_back(p, LAST, 0)
-        give_back(p, LAST, 1)
-        give_back(p, 2)
-        give_back(p, 1)
-        give_back(p, 0)
-        returned(p, 3)
-        returned(p, 4)
-        weigh(p, 6)
-        weigh(p, 5)
-        sum_fresh(p)
-        returned(p, LAST, 0)
-        weigh(p, 7, 0)
-        sum_far(p, 0)
-        returned(p, LAST, 1)
-        weigh(p, 7, 1)
-        sum_far(p, 1)
-        sum_join(p)
-        returned(p, 2)
-        weigh(p, 4)
-        weigh(p, 3)
-        sum_on(p, 2)
-        returned(p, 1)
-        returned(p, 0)
-        weigh(p, 2)
-        weigh(p, 1)
-        weigh(p, 0)
-        sum_on(p, 3)
-        finish(p)
-        if p == 0:
-            gather_start(1)
+        waited = p == 1
+        for name, i, f in PLAN:
+            if p == 0 and name == "GO" or p == 1 and name in ("MC", "M"):
+                continue
+            if name == "X" and not waited:
+                waited = True
+                for copy in weight_copies:
+                    copy.wait()
+            run(p, name, i, f)
 
     meta_wait(m_send)
     for p in (0, 1):
@@ -474,7 +448,7 @@
         compiler_params=pltpu.CompilerParams(
             collective_id=0, has_side_effects=True, vmem_limit_bytes=60 * 1024 * 1024
         ),
-    )(tokens, group_ids, expert_ids, gate_weights, w_gate, w_up, w_down)
+    )(tokens, group_ids.T, jnp.swapaxes(expert_ids, 1, 2), jnp.swapaxes(gate_weights, 1, 2), w_gate, w_up, w_down)
 
 
 def solution(mesh):

time: 153 us -> 145 us (0.948)
  local copies, waits for them, and re-layouts: 5.96 us -> 1.67 us
  Pallas kernels: 147 us -> 143 us
    unnamed x4 -> x1, local copies, waits for them, and re-layouts: 5.96 us -> 1.67 us
    pallas_call x1, Pallas kernels: 147 us -> 143 us  [on_device(): pl.pallas_call(kernel, out_shape=jax.ShapeDtypeStruct((rows, width), BF16...]
where the time goes in v3:
time: 145 us
  Pallas kernels  143 us (99%)
  local copies, waits for them, and re-layouts  1.67 us (1%)
    pallas_call x1, Pallas kernels, on_device(): pl.pallas_call(kernel, out_shape=jax.ShapeDtypeStruct((rows, width), BF16...  143 us

profile of v3, /device:TPU:1, one launch (start us, length us, event | category | flops | bytes accessed | tf_op | source)
XLA Modules:
  0.0 144.9 jit_solution(5878603198992749553)
XLA Ops:
  0.0 143.2 %shard_map.73 = bf16[128,1024]{1,0:T(8,128)(2,1)} custom-call(bf16[128,1024]{1,0:T(8,128)(2,1)} %tok_ref.1, s32[1,128]{1,0:T(1,128)} %bitcast.5, s32[2,4,128]{2,1,0:T(4,128)} %bitcast.3, bf16[2,4,128]{2,1,0:T(4,128)(2,1)} %bitcast.4, bf16[1,2048,384]{2,1,0:T(8,128)(2,1)} %wg_hbm.1, bf16[1,2048,384]{2,1,0:T(8,128)(2,1)} %wu_hbm.1, bf16[1,384,2048]{2,1,0:T(8,128)(2,1)} %wd_hbm.1), custom_call_target="tpu_custom_call" | custom-call | tf_op jit(solution)/shard_map/pallas_call | solution.py:415
  143.2 1.7 %copy.9 = bf16[128,1024]{1,0:T(8,128)(2,1)} copy(bf16[128,1024]{1,0:T(8,128)(2,1)} %shard_map.73) | data formatting | bytes 524288

commit v4 on v3

--- a/solution.py
+++ b/solution.py
@@ -32,17 +32,17 @@
 
 
 PLAN = (
-    ("GO", 0, 0), ("MC", 0, 0), ("M", 0, 0), ("G", 1, 0), ("G", 1, 1), ("G", 1, 2), ("G", 1, 3), ("C", 1, 0),
-    ("G", 2, 1), ("C", 0, 0), ("G", 2, 0), ("G", 2, 2), ("G", 2, 3), ("C", 2, 0), ("G", 3, 1), ("G", 3, 0),
-    ("C", 4, 0), ("G", 3, 2), ("L", 0, 0), ("C", 3, 0), ("G", 3, 3), ("C", 4, 1), ("L", 1, 0), ("C", 3, 1),
-    ("X", 0, 0), ("G", 4, 1), ("L", 4, 0), ("G", 4, 0), ("C", 5, 0), ("L", 4, 1), ("C", 5, 1), ("L", 3, 0),
-    ("L", 3, 1), ("X", 4, 0), ("X", 3, 0), ("B", 4, 0), ("L", 5, 0), ("B", 3, 0), ("L", 5, 1), ("L", 2, 0),
-    ("B", 4, 1), ("X", 5, 0), ("X", 2, 0), ("B", 5, 0), ("B", 5, 1), ("T", 4, 0), ("W", 6, 0), ("T", 3, 0),
-    ("W", 5, 0), ("R", 1, 3), ("B", 3, 1), ("R", 1, 2), ("X", 1, 0), ("T", 4, 1), ("B", 2, 0), ("T", 5, 0),
-    ("W", 7, 0), ("R", 0, 0), ("T", 5, 1), ("W", 7, 1), ("R", 0, 1), ("B", 1, 0), ("T", 3, 1), ("B", 0, 0),
-    ("W", 6, 1), ("W", 5, 1), ("R", 1, 0), ("R", 1, 1), ("T", 2, 0), ("W", 3, 0), ("W", 4, 0), ("R", 2, 2),
-    ("R", 2, 3), ("T", 1, 0), ("R", 2, 1), ("R", 2, 0), ("W", 2, 0), ("T", 0, 0), ("W", 1, 0), ("R", 3, 3),
-    ("R", 3, 1), ("R", 3, 0), ("R", 3, 2), ("W", 0, 0), ("F1", 0, 0), ("F2", 0, 0),
+    ("GO", 0, 0), ("G", 1, 0), ("MC", 0, 0), ("G", 1, 1), ("G", 1, 2), ("M", 0, 0), ("G", 1, 3), ("C", 0, 0),
+    ("G", 2, 0), ("C", 1, 0), ("G", 2, 1), ("G", 2, 2), ("G", 2, 3), ("C", 2, 0), ("G", 3, 1), ("G", 3, 0),
+    ("C", 4, 0), ("G", 3, 2), ("C", 3, 0), ("G", 3, 3), ("C", 4, 1), ("C", 3, 1), ("L", 2, 0), ("L", 0, 0),
+    ("G", 4, 1), ("C", 5, 1), ("X", 2, 0), ("G", 4, 0), ("L", 1, 0), ("L", 4, 0), ("L", 3, 0), ("C", 5, 0),
+    ("B", 2, 0), ("L", 4, 1), ("L", 3, 1), ("X", 4, 0), ("X", 3, 0), ("B", 4, 0), ("L", 5, 0), ("B", 3, 0),
+    ("L", 5, 1), ("B", 3, 1), ("X", 5, 0), ("X", 0, 0), ("B", 5, 1), ("B", 5, 0), ("T", 4, 0), ("W", 6, 0),
+    ("T", 3, 0), ("W", 5, 0), ("R", 1, 3), ("T", 2, 0), ("B", 4, 1), ("R", 1, 2), ("T", 3, 1), ("X", 1, 0),
+    ("T", 5, 1), ("W", 5, 1), ("W", 7, 1), ("R", 0, 1), ("W", 3, 0), ("B", 1, 0), ("T", 5, 0), ("W", 7, 0),
+    ("R", 0, 0), ("T", 4, 1), ("W", 4, 0), ("R", 2, 2), ("B", 0, 0), ("W", 6, 1), ("R", 1, 1), ("R", 1, 0),
+    ("R", 2, 3), ("T", 1, 0), ("R", 2, 1), ("T", 0, 0), ("W", 0, 0), ("R", 2, 0), ("W", 2, 0), ("W", 1, 0),
+    ("R", 3, 2), ("R", 3, 3), ("R", 3, 0), ("R", 3, 1), ("F1", 0, 0), ("F2", 0, 0),
 )
 
 
@@ -51,17 +51,18 @@
 
 
 def kernel(
-    tok_ref, gid_ref, eid_ref, gw_ref, wg_hbm, wu_hbm, wd_hbm, out_ref,
+    tok_hbm, gid_hbm, eid_hbm, gw_hbm, wg_hbm, wu_hbm, wd_hbm, out_hbm,
+    gid_ref, eid_ref, gw_ref, out_ref,
     wg, wu, wd, xa, sel, rows_in, part_out, part_in, acc, term_out, term_in, yv, ring_out, ring_in,
     meta_out, meta, lift, sq_out, sq_in,
-    w_sem, g_send, g_recv, r_send, r_recv, x_send, x_recv, t_send, t_recv, d_send, d_recv, p_send, p_recv,
+    a_sem, o_sem, w_sem, g_send, g_recv, r_send, r_recv, x_send, x_recv, t_send, t_recv, d_send, d_recv, p_send, p_recv,
     n_send, n_recv, m_send, m_recv,
 ):
     g = lax.axis_index("group")
     m = lax.axis_index("member")
     h = lax.axis_index("half")
     groups, members = 16, 8
-    rows, width = tok_ref.shape
+    rows, width = tok_hbm.shape
     cut = width // CUTS
 
     def place(group=None, member=None, half=None):
@@ -100,6 +101,17 @@
     lax.fori_loop(1, members, greet_member, 0)
     lax.fori_loop(1, groups, greet_group, 0)
 
+    row_copies = [
+        pltpu.make_async_copy(tok_hbm.at[:, pl.ds(c * cut, cut)], xa.at[0, 0, c], a_sem.at[c])
+        for c in range(CUTS)
+    ]
+    route_copies = [
+        pltpu.make_async_copy(gid_hbm, gid_ref, a_sem.at[CUTS]),
+        pltpu.make_async_copy(eid_hbm, eid_ref, a_sem.at[CUTS + 1]),
+        pltpu.make_async_copy(gw_hbm, gw_ref, a_sem.at[CUTS + 2]),
+    ]
+    for copy in row_copies + route_copies:
+        copy.start()
     own_k = pl.ds(pl.multiple_of(h * width, width), width)
     other_k = pl.ds(pl.multiple_of((1 - h) * width, width), width)
     weight_copies = [
@@ -296,6 +308,9 @@
         sq_out[p] = squares
         square_copy(p).start()
 
+    def out_copy(c):
+        return pltpu.make_async_copy(out_ref.at[c], out_hbm.at[:, lanes(c)], o_sem.at[c])
+
     def norm(p):
         square_copy(p).wait_recv()
         mean = jnp.sum(sq_out[p] + sq_in[p], axis=1, keepdims=True) / (2 * width)
@@ -305,14 +320,17 @@
             if p == 0:
                 xa[1, 0, c] = value
             else:
-                out_ref[:, lanes(c)] = value
-
-    for c in range(CUTS):
-        xa[0, 0, c] = tok_ref[:, lanes(c)]
+                out_ref[c] = value
+                out_copy(c).start()
+
+    for copy in row_copies:
+        copy.wait()
     pl.semaphore_wait(barrier, groups + members - 1)
     gather_start(0)
 
     def make_meta():
+        for copy in route_copies:
+            copy.wait()
         lane = lax.broadcasted_iota(jnp.int32, (rows, rows), 1)
         number = lax.broadcasted_iota(jnp.int32, (groups, rows), 0)
         group_of = gid_ref[...]
@@ -387,6 +405,8 @@
             run(p, name, i, f)
 
     meta_wait(m_send)
+    for c in range(CUTS):
+        out_copy(c).wait()
     for p in (0, 1):
         square_copy(p).wait_send()
         for k in range(TILES):
@@ -409,15 +429,18 @@
     cut = width // CUTS
     tile = (16, CUTS, TILE, cut)
     block = (CUTS, rows, cut)
-    vmem = pl.BlockSpec(memory_space=pltpu.VMEM)
     anywhere = pl.BlockSpec(memory_space=pl.ANY)
     dma = pltpu.SemaphoreType.DMA
     return pl.pallas_call(
         kernel,
         out_shape=jax.ShapeDtypeStruct((rows, width), BF16),
-        in_specs=[vmem] * 4 + [anywhere] * 3,
-        out_specs=vmem,
+        in_specs=[anywhere] * 7,
+        out_specs=anywhere,
         scratch_shapes=[
+            pltpu.VMEM((1, rows), jnp.int32),
+            pltpu.VMEM((2, 4, rows), jnp.int32),
+            pltpu.VMEM((2, 4, rows), BF16),
+            pltpu.VMEM(block, BF16),
             pltpu.VMEM((2, width, hidden), BF16),
             pltpu.VMEM((2, width, hidden), BF16),
             pltpu.VMEM((2, hidden, width), BF16),
@@ -437,6 +460,8 @@
             pltpu.VMEM(block, F32),
             pltpu.VMEM((2, rows, 128), F32),
             pltpu.VMEM((2, rows, 128), F32),
+            dma((CUTS + 3,)),
+            dma((CUTS,)),
             dma((6,)),
             dma((2, 4, 2, CUTS)),
             dma((2, 4, 2, CUTS)),

time: 145 us -> 143 us (0.986)
  Pallas kernels: 143 us -> 141 us
    pallas_call x1, Pallas kernels: 143 us -> 141 us  [on_device(): pl.pallas_call(kernel, out_shape=jax.ShapeDtypeStruct((rows, width), BF16...]
where the time goes in v4:
time: 143 us
  Pallas kernels  141 us (99%)
  local copies, waits for them, and re-layouts  1.67 us (1%)
    pallas_call x1, Pallas kernels, on_device(): pl.pallas_call(kernel, out_shape=jax.ShapeDtypeStruct((rows, width), BF16...  141 us

profile of v4, /device:TPU:1, one launch (start us, length us, event | category | flops | bytes accessed | tf_op | source)
XLA Modules:
  0.0 143.0 jit_solution(13481805112474769627)
XLA Ops:
  0.0 141.4 %shard_map.73 = bf16[128,1024]{1,0:T(8,128)(2,1)} custom-call(bf16[128,1024]{1,0:T(8,128)(2,1)} %tok_hbm.1, s32[1,128]{1,0:T(1,128)} %bitcast.5, s32[2,4,128]{2,1,0:T(4,128)} %bitcast.3, bf16[2,4,128]{2,1,0:T(4,128)(2,1)} %bitcast.4, bf16[1,2048,384]{2,1,0:T(8,128)(2,1)} %wg_hbm.1, bf16[1,2048,384]{2,1,0:T(8,128)(2,1)} %wu_hbm.1, bf16[1,384,2048]{2,1,0:T(8,128)(2,1)} %wd_hbm.1), custom_call_target="tpu_custom_call" | custom-call | tf_op jit(solution)/shard_map/pallas_call | solution.py:434
  141.4 1.7 %copy.9 = bf16[128,1024]{1,0:T(8,128)(2,1)} copy(bf16[128,1024]{1,0:T(8,128)(2,1)} %shard_map.73) | data formatting | bytes 524288
